TPU v7x, 32 devices: a whole 2x2x4 slice. The times are simulated.
32 devices in a mesh: mp: 2 (over x), row: 16 (over z, y, core).
Axes of the slice: x: 2, y: 2, z: 4, core: 2. Of those that a mesh axis runs over, the one named last changes fastest.
Arguments:
- radial_funcs: bfloat16 [128, 1024], P('row'), may hold values from -6 to 6
- kernels: bfloat16 [80, 1024], P('mp'), parts along dimension 0, may hold values from -0.0010299683 to 0.0010299683
- wigner: float32 [40, 128], replicated, may hold values from -4 to 4
- sources: bfloat16 [64, 2048], P('mp', 'row'), parts along dimension 0, may hold values from -6 to 6
- wigner_slots: int32 [2048], P('row'), may hold values from 0 to 127
- owners: int32 [2048], P('row'), may hold values from 0 to 7, as said below
- degrees: int32 [128], P('row'), may hold values from 0 to 30
- frequencies: float32 [2048], P('row'), may hold values from 0.5 to 2
Outputs:
- response: float32 [64, 2048], P('mp', 'row'), parts along dimension 0
There are 2 independent parts, one for each index of `mp`. A program takes and returns all parts, laid end to end along the dimension named above; an argument that names none is the same for every part. Nothing has to cross between parts.
Inputs may be any that keep to these rules, and one draw needn't show every extreme that they name: Within each aligned block of 128 singlets, owners never falls and every value 0 to 7 occurs.
All inputs are finite; a program needn't handle non-finite values.
Results may differ from a plain program's by a relative error of at most 0.0055.
Values may be sent and summed in bfloat16 or wider, within the bound.
A program may use at most 128 MiB of HBM per device.

v0:
```python
import jax
import jax.numpy as jnp
from jax import lax
from jax.sharding import PartitionSpec as P


def lookup(wigner, slot_block):
    return jnp.take(wigner, slot_block, axis=1)


def project(source_block, slot_block, owner_block, wigner, mult_dev):
    angular = lookup(wigner, slot_block)
    member = (owner_block[:, None] == jnp.arange(mult_dev, dtype=jnp.int32)[None, :]).astype(
        jnp.float32
    )
    scaled = angular[:, None, :] * source_block.astype(jnp.float32)[None, :, :]
    return jnp.einsum("skj,ja->ska", scaled, member, precision=lax.Precision.HIGHEST)


def selection(near_deg, far_deg, num_degree):
    level = jnp.arange(num_degree, dtype=jnp.int32)[:, None, None]
    total_deg = near_deg[None, :, None] + far_deg[None, None, :]
    diff_deg = jnp.abs(near_deg[None, :, None] - far_deg[None, None, :])
    return (diff_deg <= level) & (level <= total_deg) & ((total_deg + level) % 2 == 0)


def local(radial_funcs, kernels, wigner, sources, wigner_slots, owners, degrees, frequencies):
    num_degree = kernels.shape[0]
    mult_dev = radial_funcs.shape[0]
    own_part = project(sources, wigner_slots, owners, wigner, mult_dev).astype(jnp.bfloat16)
    projected, deg_all = (
        lax.all_gather(own_part, "row", axis=2, tiled=True),
        lax.all_gather(degrees, "row", axis=0, tiled=True),
    )
    weighted = (
        radial_funcs.astype(jnp.float32)[None] * kernels.astype(jnp.float32)[:, None, :]
    ).astype(jnp.bfloat16)
    weighted = weighted.reshape(num_degree * mult_dev, radial_funcs.shape[1])
    fetched = lax.all_gather(radial_funcs, "row", axis=0, tiled=True)
    piece_rows = fetched.shape[0]
    integral = lax.dot_general(
        weighted, fetched, (((1,), (1,)), ((), ())), preferred_element_type=jnp.float32
    )
    integral = integral.reshape(num_degree, mult_dev, piece_rows)
    kept_block = jnp.where(
        selection(degrees, deg_all, num_degree), integral, jnp.float32(0.0)
    ).astype(jnp.bfloat16)
    coupled = jnp.einsum("sab,skb->ska", kept_block, projected, preferred_element_type=jnp.float32)
    angular = lookup(wigner, wigner_slots)
    member = (owners[None, :] == jnp.arange(mult_dev, dtype=jnp.int32)[:, None]).astype(jnp.float32)
    spread = jnp.einsum("ska,ai->ski", coupled, member, precision=lax.Precision.HIGHEST)
    return frequencies[None, :] * sources.astype(jnp.float32) + jnp.sum(
        angular[:, None, :] * spread, axis=0
    )


def solution(mesh):
    in_specs = (
        P("row", None),
        P("mp", None),
        P(),
        P("mp", "row"),
        P("row"),
        P("row"),
        P("row"),
        P("row"),
    )
    out_specs = P("mp", "row")
    return jax.shard_map(local, mesh=mesh, in_specs=in_specs, out_specs=out_specs, check_vma=False)
```

profile of v0, /device:TPU:0, one launch (start us, length us, event | category | flops | bytes accessed | tf_op | source)
XLA Modules:
  0.0 67.7 jit_solution(15264262395300003951)
XLA Ops:
  0.0 0.8 %copy.11 = f32[40,128]{0,1:T(8,128)S(1)} copy(f32[40,128]{1,0:T(8,128)} %param.12) | data formatting | bytes 40960 | tf_op args[2]
  0.8 0.7 compare_select_fusion
  1.5 0.6 gather_fusion
  2.1 0.7 compare_and_fusion
  2.8 0.1 select_bitcast_fusion
  2.9 0.1 copy.12
  2.9 0.7 %convert_element_type.23 = f32[32,128]{1,0:T(8,128)S(1)} convert(bf16[32,128]{1,0:T(8,128)(2,1)} %param.13) | non-fusion elementwise | flops 4096 | bytes 24576 | tf_op jit(solution)/shard_map/convert_element_type | solution.py:52
  3.7 2.1 %fusion.7 = bf16[40,32,8]{1,2,0:T(8,128)(2,1)S(1)} fusion(f32[32,128]{1,0:T(8,128)S(1)} %convert_element_type.23, f32[40,128]{1,0:T(8,128)S(1)} %copy.12, s32[128]{0:T(128)} %param.15), kind=kOutput, calls=%fused_computation.9 | convolution fusion | flops 15893504 | bytes 57856 | tf_op jit(solution)/shard_map/skj,ja->ska/dot_general | solution.py:17
  5.8 0.1 copy.13
  5.9 0.0 copy-start.6
  5.9 0.0 copy-start.3
  6.0 0.0 copy-start.1
  6.0 26.2 %all_gather.9 = bf16[40,32,128]{0,1,2:T(8,128)(2,1)S(1)} all-gather(bf16[40,32,8]{0,1,2:T(8,128)(2,1)S(1)} %copy.13), channel_id=1, replica_groups=mesh['mp'=2,'row'=16] {'row'}, dimensions={2}, use_global_device_ids=true | all-gather | bytes 348160 | tf_op jit(solution)/shard_map/all_gather | solution.py:32
  32.2 0.0 copy-start
  32.2 1.4 %copy.14 = bf16[40,32,128]{2,1,0:T(8,128)(2,1)S(1)} copy(bf16[40,32,128]{0,1,2:T(8,128)(2,1)S(1)} %all_gather.9) | data formatting | bytes 655360 | tf_op jit(solution)/shard_map/all_gather | solution.py:32
  33.6 0.0 copy-done.6
  33.6 0.6 dynamic-slice
  34.8 0.0 copy-done.3
  34.8 0.2 dynamic-update-slice
  35.1 6.8 %all-reduce = s32[128]{0:T(128)S(1)} all-reduce(s32[128]{0:T(128)S(1)} %dynamic-update-slice), channel_id=1, replica_groups=mesh['mp'=2,'row'=16] {'row'}, use_global_device_ids=true, to_apply=%add | all-reduce | flops 128 | bytes 1024
  41.8 0.1 subtract_abs_fusion
  41.9 0.0 copy-done.1
  41.9 23.5 %all_gather.11 = bf16[128,1024]{1,0:T(8,128)(2,1)S(1)} all-gather(bf16[8,1024]{1,0:T(8,128)(2,1)S(1)} %copy-done.1), channel_id=1, replica_groups=mesh['mp'=2,'row'=16] {'row'}, dimensions={0}, use_global_device_ids=true | all-gather | bytes 278528 | tf_op jit(solution)/shard_map/all_gather | solution.py:39
  65.5 0.0 copy-done
  65.5 0.0 copy-start.5
  65.5 0.0 copy-start.2
  65.5 0.0 copy-start.4
  65.5 0.8 %fusion.2 = f32[40,32,8]{1,2,0:T(8,128)S(1)} fusion(bf16[40,32,128]{2,1,0:T(8,128)(2,1)S(1)} %copy.14, f32[40,1024]{1,0:T(8,128)S(1)} %convert_element_type.26, f32[8,1024]{1,0:T(8,128)S(1)} %convert_element_type.25, bf16[128,1024]{1,0:T(8,128)(2,1)S(1)} %all_gather.11, s32[8,128]{1,0:T(8,128)S(1)} %get-tuple-element.7, s32[8,128]{1,0:T(8,128)S(1)} %get-tuple-element.6), kind=kOutput, calls=%fused_computation.6 | convolution fusion | flops 87941120 | bytes 835584 | tf_op jit(solution)/shard_map/sab,skb->ska/dot_general | solution.py:48
  66.3 0.0 copy-done.5
  66.3 0.7 %fusion = f32[32,128]{1,0:T(8,128)S(1)} fusion(f32[40,32,8]{1,2,0:T(8,128)S(1)} %fusion.2, f32[40,128]{1,0:T(8,128)S(1)} %copy.12, s32[128]{0:T(128)S(1)} %copy-done.5), kind=kOutput, calls=%fused_computation.3 | convolution fusion | flops 16053248 | bytes 78336 | tf_op jit(solution)/shard_map/ska,ai->ski/dot_general | solution.py:51
  67.1 0.0 copy-done.2
  67.1 0.0 copy-done.4
  67.1 0.6 multiply_add_fusion
  (4 shorter events, 0.0 us)
Async XLA Ops:
  5.9 27.7 %copy-start.6 = (u32[32]{0:T(128)S(1)}, u32[32]{0:T(128)}, u32[]{:S(2)}) copy-start(u32[32]{0:T(128)} %constant.32) | copy-start | bytes 388
  5.9 28.9 %copy-start.3 = (s32[8]{0:T(128)S(1)}, s32[8]{0:T(128)}, u32[]{:S(2)}) copy-start(s32[8]{0:T(128)} %param.16) | copy-start | bytes 100
  6.0 36.0 %copy-start.1 = (bf16[8,1024]{1,0:T(8,128)(2,1)S(1)}, bf16[8,1024]{1,0:T(8,128)(2,1)}, u32[]{:S(2)}) copy-start(bf16[8,1024]{1,0:T(8,128)(2,1)} %param.10) | copy-start | bytes 49156
  32.2 33.3 %copy-start = (bf16[40,1024]{1,0:T(8,128)(2,1)S(1)}, bf16[40,1024]{1,0:T(8,128)(2,1)}, u32[]{:S(2)}) copy-start(bf16[40,1024]{1,0:T(8,128)(2,1)} %param.11) | copy-start | bytes 245764
  65.5 0.9 %copy-start.5 = (s32[128]{0:T(128)S(1)}, s32[128]{0:T(128)}, u32[]{:S(2)}) copy-start(s32[128]{0:T(128)} %param.15) | copy-start | bytes 1540
  65.5 1.6 %copy-start.2 = (bf16[32,128]{1,0:T(8,128)(2,1)S(1)}, bf16[32,128]{1,0:T(8,128)(2,1)}, u32[]{:S(2)}) copy-start(bf16[32,128]{1,0:T(8,128)(2,1)} %param.13) | copy-start | bytes 24580
  65.5 1.6 %copy-start.4 = (f32[128]{0:T(128)S(1)}, f32[128]{0:T(128)}, u32[]{:S(2)}) copy-start(f32[128]{0:T(128)} %param.17) | copy-start | bytes 1540
where the time goes:
time: 68 us; the launch traced here: 67.7 us
  blocking collectives  56.5 us (83%)
  local copies, waits for them, and re-layouts  3.89 us (6%)
  matrix products  3.68 us (5%)
  other arithmetic  2.84 us (4%)
  between operations  0.79 us (1%)
    all_gather x1, blocking collectives, local(): lax.all_gather(own_part, 'row', axis=2, tiled=True)  26.2 us
    all_gather x1, blocking collectives, local(): fetched = lax.all_gather(radial_funcs, 'row', axis=0, tiled=True)  23.5 us
    unnamed x1, blocking collectives  6.75 us
    dot_general x1, matrix products, project(): jnp.einsum('skj,ja->ska', scaled, member, precision=lax.Precision.HIGHEST)  2.11 us
    unnamed x17, local copies, waits for them, and re-layouts  1.69 us

commit v1 on v0

--- a/solution.py
+++ b/solution.py
@@ -36,7 +36,12 @@
         radial_funcs.astype(jnp.float32)[None] * kernels.astype(jnp.float32)[:, None, :]
     ).astype(jnp.bfloat16)
     weighted = weighted.reshape(num_degree * mult_dev, radial_funcs.shape[1])
-    fetched = lax.all_gather(radial_funcs, "row", axis=0, tiled=True)
+    ring = [radial_funcs]
+    for hop in range(15):
+        ring.append(lax.ppermute(ring[-1], "row", [(dev, (dev + 1) % 16) for dev in range(16)]))
+    fetched = jnp.roll(
+        jnp.concatenate(ring[::-1], axis=0), (lax.axis_index("row") + 1) * ring[0].shape[0], axis=0
+    )
     piece_rows = fetched.shape[0]
     integral = lax.dot_general(
         weighted, fetched, (((1,), (1,)), ((), ())), preferred_element_type=jnp.float32

time: 68 us -> 120 us (1.76)
  waiting for transfers between devices: 0 us -> 72.5 us
  blocking collectives: 56.5 us -> 33.1 us
  local copies, waits for them, and re-layouts: 3.89 us -> 5.27 us
    ppermute x0 -> x15, waiting for transfers between devices: none -> 72.5 us  [local(): lax.ppermute(ring[-1], 'row', [(dev, (dev + 1) % 16) for dev in range(16)])]
    all_gather x1 -> x0, blocking collectives: 23.5 us -> none  [local(): fetched = lax.all_gather(radial_funcs, 'row', axis=0, tiled=True)]
    unnamed x1, blocking collectives: 6.75 us -> 12.1 us
    all_gather x1, blocking collectives: 26.2 us -> 21 us  [local(): lax.all_gather(own_part, 'row', axis=2, tiled=True)]
    unnamed x17 -> x44, local copies, waits for them, and re-layouts: 1.69 us -> 3.08 us
  transfers between devices with their start and end apart: 0 -> 15, of which waited for: 0 -> 13; matrix products, arithmetic and copies ran while one was open for 0% -> 8% of each run, Pallas kernels for 0% -> 0%
where the time goes in v1:
time: 120 us
  waiting for transfers between devices  72.5 us (60%)
  blocking collectives  33.1 us (28%)
  local copies, waits for them, and re-layouts  5.27 us (4%)
  matrix products  3.69 us (3%)
  other arithmetic  3.47 us (3%)
    ppermute x15, waiting for transfers between devices, local(): lax.ppermute(ring[-1], 'row', [(dev, (dev + 1) % 16) for dev in range(16)])  72.5 us
    all_gather x1, blocking collectives, local(): lax.all_gather(own_part, 'row', axis=2, tiled=True)  21 us
    unnamed x1, blocking collectives  12.1 us
    unnamed x44, local copies, waits for them, and re-layouts  3.08 us
  transfers between devices with their start and end apart: 15, of which 13 were waited for; matrix products, arithmetic and copies ran while one was open for 8% of the time, Pallas kernels for 0%

profile of v1, /device:TPU:0, one launch (start us, length us, event | category | flops | bytes accessed | tf_op | source)
XLA Modules:
  0.0 119.5 jit_solution(13592515726232305999)
XLA Ops:
  0.0 0.5 collective-permute-start
  0.5 6.6 %collective-permute-done = bf16[8,1024]{1,0:T(8,128)(2,1)S(1)} collective-permute-done((bf16[8,1024]{1,0:T(8,128)(2,1)}, bf16[8,1024]{1,0:T(8,128)(2,1)S(1)}, u32[]{:S(2)}, u32[]{:S(2)}) %collective-permute-start) | collective-permute-done | bytes 16416 | tf_op jit(solution)/shard_map/ppermute | solution.py:41
  7.1 0.0 collective-permute-start.1
  7.1 5.9 %collective-permute-done.1 = bf16[8,1024]{1,0:T(8,128)(2,1)S(1)} collective-permute-done((bf16[8,1024]{1,0:T(8,128)(2,1)S(1)}, bf16[8,1024]{1,0:T(8,128)(2,1)S(1)}, u32[]{:S(2)}, u32[]{:S(2)}) %collective-permute-start.1) | collective-permute-done | bytes 16416 | tf_op jit(solution)/shard_map/ppermute | solution.py:41
  12.9 0.0 collective-permute-start.2
  12.9 5.9 %collective-permute-done.2 = bf16[8,1024]{1,0:T(8,128)(2,1)S(1)} collective-permute-done((bf16[8,1024]{1,0:T(8,128)(2,1)S(1)}, bf16[8,1024]{1,0:T(8,128)(2,1)S(1)}, u32[]{:S(2)}, u32[]{:S(2)}) %collective-permute-start.2) | collective-permute-done | bytes 16416 | tf_op jit(solution)/shard_map/ppermute | solution.py:41
  18.8 0.0 collective-permute-start.3
  18.8 5.9 %collective-permute-done.3 = bf16[8,1024]{1,0:T(8,128)(2,1)S(1)} collective-permute-done((bf16[8,1024]{1,0:T(8,128)(2,1)S(1)}, bf16[8,1024]{1,0:T(8,128)(2,1)S(1)}, u32[]{:S(2)}, u32[]{:S(2)}) %collective-permute-start.3) | collective-permute-done | bytes 16416 | tf_op jit(solution)/shard_map/ppermute | solution.py:41
  24.7 0.0 collective-permute-start.4
  24.7 5.9 %collective-permute-done.4 = bf16[8,1024]{1,0:T(8,128)(2,1)S(1)} collective-permute-done((bf16[8,1024]{1,0:T(8,128)(2,1)S(1)}, bf16[8,1024]{1,0:T(8,128)(2,1)S(1)}, u32[]{:S(2)}, u32[]{:S(2)}) %collective-permute-start.4) | collective-permute-done | bytes 16416 | tf_op jit(solution)/shard_map/ppermute | solution.py:41
  30.5 0.0 collective-permute-start.5
  30.5 5.9 %collective-permute-done.5 = bf16[8,1024]{1,0:T(8,128)(2,1)S(1)} collective-permute-done((bf16[8,1024]{1,0:T(8,128)(2,1)S(1)}, bf16[8,1024]{1,0:T(8,128)(2,1)S(1)}, u32[]{:S(2)}, u32[]{:S(2)}) %collective-permute-start.5) | collective-permute-done | bytes 16416 | tf_op jit(solution)/shard_map/ppermute | solution.py:41
  36.4 0.0 collective-permute-start.6
  36.4 5.9 %collective-permute-done.6 = bf16[8,1024]{1,0:T(8,128)(2,1)S(1)} collective-permute-done((bf16[8,1024]{1,0:T(8,128)(2,1)S(1)}, bf16[8,1024]{1,0:T(8,128)(2,1)S(1)}, u32[]{:S(2)}, u32[]{:S(2)}) %collective-permute-start.6) | collective-permute-done | bytes 16416 | tf_op jit(solution)/shard_map/ppermute | solution.py:41
  42.2 0.0 collective-permute-start.7
  42.2 5.9 %collective-permute-done.7 = bf16[8,1024]{1,0:T(8,128)(2,1)S(1)} collective-permute-done((bf16[8,1024]{1,0:T(8,128)(2,1)S(1)}, bf16[8,1024]{1,0:T(8,128)(2,1)S(1)}, u32[]{:S(2)}, u32[]{:S(2)}) %collective-permute-start.7) | collective-permute-done | bytes 16416 | tf_op jit(solution)/shard_map/ppermute | solution.py:41
  48.1 0.0 collective-permute-start.8
  48.1 0.7 compare_select_fusion
  48.8 5.2 %collective-permute-done.8 = bf16[8,1024]{1,0:T(8,128)(2,1)S(1)} collective-permute-done((bf16[8,1024]{1,0:T(8,128)(2,1)S(1)}, bf16[8,1024]{1,0:T(8,128)(2,1)S(1)}, u32[]{:S(2)}, u32[]{:S(2)}) %collective-permute-start.8) | collective-permute-done | bytes 16416 | tf_op jit(solution)/shard_map/ppermute | solution.py:41
  54.0 0.0 collective-permute-start.9
  54.0 0.7 compare_and_fusion
  54.6 5.2 %collective-permute-done.9 = bf16[8,1024]{1,0:T(8,128)(2,1)S(1)} collective-permute-done((bf16[8,1024]{1,0:T(8,128)(2,1)S(1)}, bf16[8,1024]{1,0:T(8,128)(2,1)S(1)}, u32[]{:S(2)}, u32[]{:S(2)}) %collective-permute-start.9) | collective-permute-done | bytes 16416 | tf_op jit(solution)/shard_map/ppermute | solution.py:41
  59.8 0.0 collective-permute-start.10
  59.8 0.8 copy.11
  60.7 0.6 gather_fusion
  61.3 4.4 %collective-permute-done.10 = bf16[8,1024]{1,0:T(8,128)(2,1)S(1)} collective-permute-done((bf16[8,1024]{1,0:T(8,128)(2,1)S(1)}, bf16[8,1024]{1,0:T(8,128)(2,1)S(1)}, u32[]{:S(2)}, u32[]{:S(2)}) %collective-permute-start.10) | collective-permute-done | bytes 16416 | tf_op jit(solution)/shard_map/ppermute | solution.py:41
  65.7 0.0 collective-permute-start.11
  65.7 0.1 select_bitcast_fusion
  65.8 0.7 convert_element_type.23
  66.5 0.1 copy.12
  66.5 5.0 %collective-permute-done.11 = bf16[8,1024]{1,0:T(8,128)(2,1)S(1)} collective-permute-done((bf16[8,1024]{1,0:T(8,128)(2,1)S(1)}, bf16[8,1024]{1,0:T(8,128)(2,1)S(1)}, u32[]{:S(2)}, u32[]{:S(2)}) %collective-permute-start.11) | collective-permute-done | bytes 16416 | tf_op jit(solution)/shard_map/ppermute | solution.py:41
  71.6 0.0 collective-permute-start.12
  71.6 2.1 %fusion.7 = bf16[40,32,8]{1,2,0:T(8,128)(2,1)S(1)} fusion(f32[32,128]{1,0:T(8,128)S(1)} %convert_element_type.23, f32[40,128]{1,0:T(8,128)S(1)} %copy.12, s32[128]{0:T(128)} %param.15), kind=kOutput, calls=%fused_computation.9 | convolution fusion | flops 15893504 | bytes 57856 | tf_op jit(solution)/shard_map/skj,ja->ska/dot_general | solution.py:17
  73.7 1.3 %dynamic-slice = u32[1]{0:T(128)} dynamic-slice(u32[32]{0:T(128)} %constant.60, u32[]{:T(128)S(6)} %add.58), dynamic_slice_sizes={1} | dynamic-slice | bytes 12
  75.6 0.9 dynamic-update-slice
  76.4 12.1 %all-reduce = s32[128]{0:T(128)S(1)} all-reduce(s32[128]{0:T(128)S(1)} %dynamic-update-slice), channel_id=1, replica_groups=mesh['mp'=2,'row'=16] {'row'}, use_global_device_ids=true, to_apply=%add | all-reduce | flops 128 | bytes 1024
  88.5 0.0 collective-permute-done.12
  88.5 0.0 collective-permute-start.13
  88.5 0.7 subtract_abs_fusion
  89.3 0.1 copy.13
  89.4 0.0 copy-start
  89.4 5.1 %collective-permute-done.13 = bf16[8,1024]{1,0:T(8,128)(2,1)S(1)} collective-permute-done((bf16[8,1024]{1,0:T(8,128)(2,1)S(1)}, bf16[8,1024]{1,0:T(8,128)(2,1)S(1)}, u32[]{:S(2)}, u32[]{:S(2)}) %collective-permute-start.13) | collective-permute-done | bytes 16416 | tf_op jit(solution)/shard_map/ppermute | solution.py:41
  94.5 0.0 collective-permute-start.14
  94.5 21.0 %all_gather.6 = bf16[40,32,128]{0,1,2:T(8,128)(2,1)S(1)} all-gather(bf16[40,32,8]{0,1,2:T(8,128)(2,1)S(1)} %copy.13), channel_id=1, replica_groups=mesh['mp'=2,'row'=16] {'row'}, dimensions={2}, use_global_device_ids=true | all-gather | bytes 348160 | tf_op jit(solution)/shard_map/all_gather | solution.py:32
  115.5 0.0 copy-start.1
  115.5 1.4 %copy.14 = bf16[40,32,128]{2,1,0:T(8,128)(2,1)S(1)} copy(bf16[40,32,128]{0,1,2:T(8,128)(2,1)S(1)} %all_gather.6) | data formatting | bytes 655360 | tf_op jit(solution)/shard_map/all_gather | solution.py:32
  116.8 0.0 copy-done
  116.9 0.0 collective-permute-done.14
  117.1 0.0 copy-done.1
  117.2 0.0 copy-start.4
  117.3 0.0 copy-start.2
  117.3 0.0 copy-start.3
  117.3 0.8 fusion.2
  118.2 0.0 copy-done.4
  118.2 0.7 fusion
  118.9 0.0 copy-done.2
  118.9 0.0 copy-done.3
  118.9 0.6 multiply_add_fusion
  (35 shorter events, 0.1 us)
Async XLA Ops:
  0.0 7.1 %collective-permute-start = (bf16[8,1024]{1,0:T(8,128)(2,1)}, bf16[8,1024]{1,0:T(8,128)(2,1)S(1)}, u32[]{:S(2)}, u32[]{:S(2)}) collective-permute-start(bf16[8,1024]{1,0:T(8,128)(2,1)} %param.10), channel_id=1, source_target_pairs={{0,1},{1,2},{2,3},{3,4},{4,5},{5,6},{6,7},{7,8},{8,9},{9,10},{10,1... | collective-permute-start | bytes 49160 | tf_op jit(solution)/shard_map/ppermute | solution.py:41
  7.1 5.9 %collective-permute-start.1 = (bf16[8,1024]{1,0:T(8,128)(2,1)S(1)}, bf16[8,1024]{1,0:T(8,128)(2,1)S(1)}, u32[]{:S(2)}, u32[]{:S(2)}) collective-permute-start(bf16[8,1024]{1,0:T(8,128)(2,1)S(1)} %collective-permute-done), channel_id=1, source_target_pairs={{0,1},{1,2},{2,3},{3,4},{4,5},{5,6},{6,7},{7,8},{8,9},{9,10},{10,1... | collective-permute-start | bytes 49160 | tf_op jit(solution)/shard_map/ppermute | solution.py:41
  12.9 5.9 %collective-permute-start.2 = (bf16[8,1024]{1,0:T(8,128)(2,1)S(1)}, bf16[8,1024]{1,0:T(8,128)(2,1)S(1)}, u32[]{:S(2)}, u32[]{:S(2)}) collective-permute-start(bf16[8,1024]{1,0:T(8,128)(2,1)S(1)} %collective-permute-done.1), channel_id=1, source_target_pairs={{0,1},{1,2},{2,3},{3,4},{4,5},{5,6},{6,7},{7,8},{8,9},{9,10},{10,1... | collective-permute-start | bytes 49160 | tf_op jit(solution)/shard_map/ppermute | solution.py:41
  18.8 5.9 %collective-permute-start.3 = (bf16[8,1024]{1,0:T(8,128)(2,1)S(1)}, bf16[8,1024]{1,0:T(8,128)(2,1)S(1)}, u32[]{:S(2)}, u32[]{:S(2)}) collective-permute-start(bf16[8,1024]{1,0:T(8,128)(2,1)S(1)} %collective-permute-done.2), channel_id=1, source_target_pairs={{0,1},{1,2},{2,3},{3,4},{4,5},{5,6},{6,7},{7,8},{8,9},{9,10},{10,1... | collective-permute-start | bytes 49160 | tf_op jit(solution)/shard_map/ppermute | solution.py:41
  24.7 5.9 %collective-permute-start.4 = (bf16[8,1024]{1,0:T(8,128)(2,1)S(1)}, bf16[8,1024]{1,0:T(8,128)(2,1)S(1)}, u32[]{:S(2)}, u32[]{:S(2)}) collective-permute-start(bf16[8,1024]{1,0:T(8,128)(2,1)S(1)} %collective-permute-done.3), channel_id=1, source_target_pairs={{0,1},{1,2},{2,3},{3,4},{4,5},{5,6},{6,7},{7,8},{8,9},{9,10},{10,1... | collective-permute-start | bytes 49160 | tf_op jit(solution)/shard_map/ppermute | solution.py:41
  30.5 5.9 %collective-permute-start.5 = (bf16[8,1024]{1,0:T(8,128)(2,1)S(1)}, bf16[8,1024]{1,0:T(8,128)(2,1)S(1)}, u32[]{:S(2)}, u32[]{:S(2)}) collective-permute-start(bf16[8,1024]{1,0:T(8,128)(2,1)S(1)} %collective-permute-done.4), channel_id=1, source_target_pairs={{0,1},{1,2},{2,3},{3,4},{4,5},{5,6},{6,7},{7,8},{8,9},{9,10},{10,1... | collective-permute-start | bytes 49160 | tf_op jit(solution)/shard_map/ppermute | solution.py:41
  36.4 5.9 %collective-permute-start.6 = (bf16[8,1024]{1,0:T(8,128)(2,1)S(1)}, bf16[8,1024]{1,0:T(8,128)(2,1)S(1)}, u32[]{:S(2)}, u32[]{:S(2)}) collective-permute-start(bf16[8,1024]{1,0:T(8,128)(2,1)S(1)} %collective-permute-done.5), channel_id=1, source_target_pairs={{0,1},{1,2},{2,3},{3,4},{4,5},{5,6},{6,7},{7,8},{8,9},{9,10},{10,1... | collective-permute-start | bytes 49160 | tf_op jit(solution)/shard_map/ppermute | solution.py:41
  42.2 5.9 %collective-permute-start.7 = (bf16[8,1024]{1,0:T(8,128)(2,1)S(1)}, bf16[8,1024]{1,0:T(8,128)(2,1)S(1)}, u32[]{:S(2)}, u32[]{:S(2)}) collective-permute-start(bf16[8,1024]{1,0:T(8,128)(2,1)S(1)} %collective-permute-done.6), channel_id=1, source_target_pairs={{0,1},{1,2},{2,3},{3,4},{4,5},{5,6},{6,7},{7,8},{8,9},{9,10},{10,1... | collective-permute-start | bytes 49160 | tf_op jit(solution)/shard_map/ppermute | solution.py:41
  48.1 5.9 %collective-permute-start.8 = (bf16[8,1024]{1,0:T(8,128)(2,1)S(1)}, bf16[8,1024]{1,0:T(8,128)(2,1)S(1)}, u32[]{:S(2)}, u32[]{:S(2)}) collective-permute-start(bf16[8,1024]{1,0:T(8,128)(2,1)S(1)} %collective-permute-done.7), channel_id=1, source_target_pairs={{0,1},{1,2},{2,3},{3,4},{4,5},{5,6},{6,7},{7,8},{8,9},{9,10},{10,1... | collective-permute-start | bytes 49160 | tf_op jit(solution)/shard_map/ppermute | solution.py:41
  54.0 5.9 %collective-permute-start.9 = (bf16[8,1024]{1,0:T(8,128)(2,1)S(1)}, bf16[8,1024]{1,0:T(8,128)(2,1)S(1)}, u32[]{:S(2)}, u32[]{:S(2)}) collective-permute-start(bf16[8,1024]{1,0:T(8,128)(2,1)S(1)} %collective-permute-done.8), channel_id=1, source_target_pairs={{0,1},{1,2},{2,3},{3,4},{4,5},{5,6},{6,7},{7,8},{8,9},{9,10},{10,1... | collective-permute-start | bytes 49160 | tf_op jit(solution)/shard_map/ppermute | solution.py:41
  59.8 5.9 %collective-permute-start.10 = (bf16[8,1024]{1,0:T(8,128)(2,1)S(1)}, bf16[8,1024]{1,0:T(8,128)(2,1)S(1)}, u32[]{:S(2)}, u32[]{:S(2)}) collective-permute-start(bf16[8,1024]{1,0:T(8,128)(2,1)S(1)} %collective-permute-done.9), channel_id=1, source_target_pairs={{0,1},{1,2},{2,3},{3,4},{4,5},{5,6},{6,7},{7,8},{8,9},{9,10},{10,1... | collective-permute-start | bytes 49160 | tf_op jit(solution)/shard_map/ppermute | solution.py:41
  65.7 5.9 %collective-permute-start.11 = (bf16[8,1024]{1,0:T(8,128)(2,1)S(1)}, bf16[8,1024]{1,0:T(8,128)(2,1)S(1)}, u32[]{:S(2)}, u32[]{:S(2)}) collective-permute-start(bf16[8,1024]{1,0:T(8,128)(2,1)S(1)} %collective-permute-done.10), channel_id=1, source_target_pairs={{0,1},{1,2},{2,3},{3,4},{4,5},{5,6},{6,7},{7,8},{8,9},{9,10},{10,1... | collective-permute-start | bytes 49160 | tf_op jit(solution)/shard_map/ppermute | solution.py:41
  71.6 17.0 %collective-permute-start.12 = (bf16[8,1024]{1,0:T(8,128)(2,1)S(1)}, bf16[8,1024]{1,0:T(8,128)(2,1)S(1)}, u32[]{:S(2)}, u32[]{:S(2)}) collective-permute-start(bf16[8,1024]{1,0:T(8,128)(2,1)S(1)} %collective-permute-done.11), channel_id=1, source_target_pairs={{0,1},{1,2},{2,3},{3,4},{4,5},{5,6},{6,7},{7,8},{8,9},{9,10},{10,1... | collective-permute-start | bytes 49160 | tf_op jit(solution)/shard_map/ppermute | solution.py:41
  88.5 6.0 %collective-permute-start.13 = (bf16[8,1024]{1,0:T(8,128)(2,1)S(1)}, bf16[8,1024]{1,0:T(8,128)(2,1)S(1)}, u32[]{:S(2)}, u32[]{:S(2)}) collective-permute-start(bf16[8,1024]{1,0:T(8,128)(2,1)S(1)} %collective-permute-done.12), channel_id=1, source_target_pairs={{0,1},{1,2},{2,3},{3,4},{4,5},{5,6},{6,7},{7,8},{8,9},{9,10},{10,1... | collective-permute-start | bytes 49160 | tf_op jit(solution)/shard_map/ppermute | solution.py:41
  89.4 27.5 %copy-start = (bf16[40,1024]{1,0:T(8,128)(2,1)S(1)}, bf16[40,1024]{1,0:T(8,128)(2,1)}, u32[]{:S(2)}) copy-start(bf16[40,1024]{1,0:T(8,128)(2,1)} %param.11) | copy-start | bytes 245764
  94.5 22.4 %collective-permute-start.14 = (bf16[8,1024]{1,0:T(8,128)(2,1)S(1)}, bf16[8,1024]{1,0:T(8,128)(2,1)S(1)}, u32[]{:S(2)}, u32[]{:S(2)}) collective-permute-start(bf16[8,1024]{1,0:T(8,128)(2,1)S(1)} %collective-permute-done.13), channel_id=1, source_target_pairs={{0,1},{1,2},{2,3},{3,4},{4,5},{5,6},{6,7},{7,8},{8,9},{9,10},{10,1... | collective-permute-start | bytes 49160 | tf_op jit(solution)/shard_map/ppermute | solution.py:41
  115.5 1.6 %copy-start.1 = (bf16[8,1024]{1,0:T(8,128)(2,1)S(1)}, bf16[8,1024]{1,0:T(8,128)(2,1)}, u32[]{:S(2)}) copy-start(bf16[8,1024]{1,0:T(8,128)(2,1)} %param.10) | copy-start | bytes 49156
  117.2 0.9 copy-start.4
  117.3 1.6 %copy-start.2 = (bf16[32,128]{1,0:T(8,128)(2,1)S(1)}, bf16[32,128]{1,0:T(8,128)(2,1)}, u32[]{:S(2)}) copy-start(bf16[32,128]{1,0:T(8,128)(2,1)} %param.13) | copy-start | bytes 24580
  117.3 1.6 %copy-start.3 = (f32[128]{0:T(128)S(1)}, f32[128]{0:T(128)}, u32[]{:S(2)}) copy-start(f32[128]{0:T(128)} %param.17) | copy-start | bytes 1540
